TPU v7x, 512 devices: a whole 4x8x8 slice. The times are simulated.
512 devices in a mesh: sample: 64 (over z, x, core), basis: 8 (over y).
Axes of the slice: x: 4, y: 8, z: 8, core: 2. Of those that a mesh axis runs over, the one named last changes fastest.
Arguments:
- points: float32 [10, 131072], P(None, 'sample'), may hold values from -1 to 1
- run_weights: float32 [131072], P('sample'), may hold values from 0.25 to 6.1
- panel_degrees: int32 [10, 128], P(None, 'basis'), may hold values from 0 to 6, as said below
- trailing_degrees: int32 [10, 2048], P(None, 'basis'), may hold values from 0 to 6, as said below
Outputs:
- r_factor: float32 [128, 128], replicated
- coupling: float32 [128, 2048], P(None, 'basis')
- updated: float32 [131072, 2048], P('sample', 'basis')
Inputs may be any that keep to these rules, and one draw needn't show every extreme that they name: `panel_degrees`: every column is a multi-index of total degree at most 6; all 2176 columns are distinct. `trailing_degrees`: as for panel_degrees; no trailing column repeats a panel column.
All inputs are finite; a program needn't handle non-finite values.
Results may differ from a plain program's by a relative error of at most 0.0003.
Values sent between devices are 32-bit elements; how exact they have to be, the bound alone decides.
A program may use at most 64 MiB of HBM per device.

v0:
```python
import math
import jax
import jax.numpy as jnp
from jax import lax
from jax.sharding import PartitionSpec as P

DEG = 6


def legendre_rows(coord):
    values = [jnp.ones_like(coord), coord]
    for degree in range(1, DEG):
        values.append(
            ((2.0 * degree + 1.0) * coord * values[degree] - degree * values[degree - 1])
            / (degree + 1.0)
        )
    return jnp.stack(
        [values[degree] * math.sqrt(2.0 * degree + 1.0) for degree in range(DEG + 1)], axis=0
    )


def weighted_columns(points, degrees, weights, run_total):
    levels = jnp.arange(DEG + 1, dtype=jnp.int32)
    product = jnp.broadcast_to(
        jnp.sqrt(weights / run_total)[:, None], (weights.shape[0], degrees.shape[1])
    )
    for dim_index in range(points.shape[0]):
        table = legendre_rows(points[dim_index])
        selector = (degrees[dim_index][None, :] == levels[:, None]).astype(jnp.float32)
        product = product * lax.dot_general(
            table, selector, (((0,), (0,)), ((), ())), precision=lax.Precision.HIGHEST
        )
    return product


def inner_products(left, right):
    return lax.dot_general(left, right, (((0,), (0,)), ((), ())), precision=lax.Precision.HIGHEST)


def shards(points, run_weights, panel_degrees, trailing_degrees):
    run_count = points.shape[1] * lax.axis_size("sample")
    run_total = float(run_count)
    own_columns = weighted_columns(points, panel_degrees, run_weights, run_total)
    panel = lax.all_gather(own_columns, "basis", axis=1, tiled=True)
    trailing = weighted_columns(points, trailing_degrees, run_weights, run_total)
    width = panel.shape[1]
    identity = jnp.eye(width, dtype=jnp.float32)
    gram_matrix = lax.psum(inner_products(panel, panel), "sample")
    lower_factor = jnp.linalg.cholesky(gram_matrix)
    inverse_lower = jax.scipy.linalg.solve_triangular(lower_factor, identity, lower=True)
    ortho_rows = lax.dot_general(
        inverse_lower, panel, (((1,), (1,)), ((), ())), precision=lax.Precision.HIGHEST
    )
    local_terms = jnp.dot(ortho_rows, trailing, precision=lax.Precision.HIGHEST)
    coupling = lax.psum(local_terms, "sample")
    updated = (trailing - inner_products(ortho_rows, coupling)) * math.sqrt(run_count)
    return (lower_factor.T, coupling, updated)


def solution(mesh):
    in_specs = (P(None, "sample"), P("sample"), P(None, "basis"), P(None, "basis"))
    out_specs = (P(), P(None, "basis"), P("sample", "basis"))
    return jax.shard_map(shards, mesh=mesh, in_specs=in_specs, out_specs=out_specs, check_vma=False)
```

profile of v0, /device:TPU:1, one launch (start us, length us, event | category | flops | bytes accessed | tf_op | source)
XLA Modules:
  0.0 468.8 jit_solution(5039410544258902816)
XLA Ops:
  7.2 1.5 broadcast_multiply_fusion.40
  8.7 2.1 subtract_multiply_fusion
  10.8 1.0 slice_bitcast_fusion
  17.5 1.2 convolution_multiply_fusion.9
  18.7 1.0 convolution_multiply_fusion.8
  19.7 1.0 convolution_multiply_fusion.7
  20.8 1.0 convolution_multiply_fusion.6
  21.8 1.0 convolution_multiply_fusion.5
  22.9 1.0 convolution_multiply_fusion.4
  23.9 1.0 convolution_multiply_fusion.3
  25.0 1.0 convolution_multiply_fusion.2
  26.0 2.4 convolution_multiply_fusion.1
  28.4 30.6 %all-gather.2.cloned.1.call-done = f32[2048,128]{0,1:T(8,128)} async-done(((f32[2048,16]{0,1:T(8,128)}), f32[2048,128]{0,1:T(8,128)}) %all-gather.2.cloned.1.call-update) | async-done | bytes 1048592 | tf_op jit(solution)/shard_map/all_gather | solution.py:44
  59.0 3.2 fusion.36
  62.5 2.7 convolution_multiply_fusion
  65.2 181.5 %all-reduce.3.cloned.1.call-done = f32[128,128]{0,1:T(8,128)} async-done(((f32[128,128]{0,1:T(8,128)}), f32[128,128]{0,1:T(8,128)}) %all-reduce.3.cloned.1.call-update) | async-done | bytes 65552 | tf_op jit(solution)/shard_map/psum | solution.py:48
  246.7 0.9 copy.8
  248.5 11.7 %cholesky.20 = f32[128,128]{1,0:T(8,128)S(1)} custom-call(f32[128,128]{1,0:T(8,128)S(1)} %fusion.3), custom_call_target="Cholesky" | custom-call | tf_op jit(solution)/shard_map/jit(cholesky)/cholesky | solution.py:49
  261.6 9.8 %custom-call.7 = f32[1,128,128]{1,2,0:T(8,128)S(1)} custom-call(f32[1,128,128]{2,1,0:T(8,128)S(1)} %get-tuple-element.102), custom_call_target="InvertDiagBlocksLowerTriangular" | custom-call | tf_op jit(solution)/shard_map/jit(_solve_triangular)/triangular_solve | solution.py:50
  271.6 1.0 fusion.37
  272.7 1.0 copy-done.1
  273.6 1.8 fusion.38
  276.2 181.0 %all-reduce.5.cloned.1.call-done = f32[128,256]{1,0:T(8,128)} async-done(((f32[128,256]{1,0:T(8,128)}), f32[128,256]{1,0:T(8,128)}) %all-reduce.5.cloned.1.call-update) | async-done | bytes 131088 | tf_op jit(solution)/shard_map/psum | solution.py:55
  457.2 4.4 fusion
  (58 shorter events, 9.6 us)
Async XLA Ops:
  7.2 51.9 %all-gather.2.cloned.1.call-start = ((), (), s32[]{:S(2)}) async-start(), calls=%async_computation | async-start | bytes 1179648 | tf_op jit(solution)/shard_map/all_gather | solution.py:44
  13.4 4.1 copy-start.3
  17.2 229.5 %all-reduce.3.cloned.1.call-start = ((), (), s32[]{:S(2)}) async-start(), calls=%async_computation.1 | async-start | bytes 131072 | tf_op jit(solution)/shard_map/psum | solution.py:48
  62.2 394.9 %all-reduce.5.cloned.1.call-start = ((), (), s32[]{:S(2)}) async-start(), calls=%async_computation.2 | async-start | bytes 262144 | tf_op jit(solution)/shard_map/psum | solution.py:55
  62.5 209.1 %copy-start = (f32[2048,128]{0,1:T(8,128)S(1)}, f32[2048,128]{0,1:T(8,128)}, u32[]{:S(2)}) copy-start(f32[2048,128]{0,1:T(8,128)} %all-gather.2.cloned.1.call-done) | copy-start | bytes 3145732
  272.6 1.0 copy-start.1
  457.1 4.4 copy-start.2
Sparse Core Ops, SparseCore 0:
  17.3 41.6 all-gather.1
  63.1 183.6 all-reduce.2
  275.6 181.5 all-reduce.4
where the time goes:
time: 469 us
  waiting for transfers between devices  393 us (84%)
  other arithmetic  28.3 us (6%)
  matrix products  27.5 us (6%)
  between operations  14.1 us (3%)
  local copies, waits for them, and re-layouts  5.28 us (1%)
    psum x1, waiting for transfers between devices, shards(): gram_matrix = lax.psum(inner_products(panel, panel), 'sample')  181 us
    psum x1, waiting for transfers between devices, shards(): coupling = lax.psum(local_terms, 'sample')  181 us
    all_gather x1, waiting for transfers between devices, shards(): panel = lax.all_gather(own_columns, 'basis', axis=1, tiled=True)  30.6 us
    dot_general x20, matrix products, weighted_columns(): lax.dot_general(table, selector, (((0,), (0,)), ((), ())), precision=lax....  16.8 us
    another operation x3, other arithmetic, shards(): lower_factor = jnp.linalg.cholesky(gram_matrix)  12.4 us
    another operation x2, other arithmetic, shards(): jax.scipy.linalg.solve_triangular(lower_factor, identity, lower=True)  10.5 us
  transfers between devices with their start and end apart: 3, of which 3 were waited for; matrix products, arithmetic and copies ran while one was open for 3% of the time, Pallas kernels for 0%

commit v1 on v0

--- a/solution.py
+++ b/solution.py
@@ -45,7 +45,7 @@
     trailing = weighted_columns(points, trailing_degrees, run_weights, run_total)
     width = panel.shape[1]
     identity = jnp.eye(width, dtype=jnp.float32)
-    gram_matrix = lax.psum(inner_products(panel, panel), "sample")
+    gram_matrix = jnp.sum(lax.all_gather(inner_products(panel, panel), "sample"), axis=0)
     lower_factor = jnp.linalg.cholesky(gram_matrix)
     inverse_lower = jax.scipy.linalg.solve_triangular(lower_factor, identity, lower=True)
     ortho_rows = lax.dot_general(

time: 469 us -> 376 us (0.80)
  waiting for transfers between devices: 393 us -> 302 us
    psum x1 -> x0, waiting for transfers between devices: 181 us -> none  [shards(): gram_matrix = lax.psum(inner_products(panel, panel), 'sample')]
    all_gather x0 -> x1, waiting for transfers between devices: none -> 79 us  [shards(): lax.all_gather(inner_products(panel, panel), 'sample')]
    all_gather x1, waiting for transfers between devices: 30.6 us -> 41.7 us  [shards(): panel = lax.all_gather(own_columns, 'basis', axis=1, tiled=True)]
where the time goes in v1:
time: 376 us; the launch traced here: 375 us
  waiting for transfers between devices  302 us (80%)
  other arithmetic  30.1 us (8%)
  matrix products  24.5 us (7%)
  between operations  14.1 us (4%)
  local copies, waits for them, and re-layouts  4.45 us (1%)
    psum x1, waiting for transfers between devices, shards(): coupling = lax.psum(local_terms, 'sample')  181 us
    all_gather x1, waiting for transfers between devices, shards(): lax.all_gather(inner_products(panel, panel), 'sample')  79 us
    all_gather x1, waiting for transfers between devices, shards(): panel = lax.all_gather(own_columns, 'basis', axis=1, tiled=True)  41.7 us
    dot_general x20, matrix products, weighted_columns(): lax.dot_general(table, selector, (((0,), (0,)), ((), ())), precision=lax....  13.8 us
    another operation x3, other arithmetic, shards(): lower_factor = jnp.linalg.cholesky(gram_matrix)  12.6 us
    another operation x2, other arithmetic, shards(): jax.scipy.linalg.solve_triangular(lower_factor, identity, lower=True)  10.5 us
    dot_general x2, matrix products, inner_products(): lax.dot_general(left, right, (((0,), (0,)), ((), ())), precision=lax.Prec...  7.58 us
  transfers between devices with their start and end apart: 3, of which 3 were waited for; matrix products, arithmetic and copies ran while one was open for 3% of the time, Pallas kernels for 0%

profile of v1, /device:TPU:1, one launch (start us, length us, event | category | flops | bytes accessed | tf_op | source)
XLA Modules:
  0.0 375.3 jit_solution(17646120299408258609)
XLA Ops:
  7.2 1.5 broadcast_multiply_fusion.40
  8.7 2.1 subtract_multiply_fusion
  11.5 1.0 slice_bitcast_fusion
  17.2 41.7 %all-gather.4.cloned.1.call-done = f32[2048,128]{0,1:T(8,128)} async-done(((f32[2048,16]{0,1:T(8,128)}), f32[2048,128]{0,1:T(8,128)}) %all-gather.4.cloned.1.call-update) | async-done | bytes 1048592 | tf_op jit(solution)/shard_map/all_gather | solution.py:44
  59.0 3.2 fusion.36
  62.4 1.2 convolution_multiply_fusion.9
  63.6 1.0 convolution_multiply_fusion.8
  64.7 1.0 convolution_multiply_fusion.7
  65.7 1.0 convolution_multiply_fusion.6
  66.8 1.0 convolution_multiply_fusion.5
  67.8 1.0 convolution_multiply_fusion.4
  68.9 1.0 convolution_multiply_fusion.3
  70.0 1.0 convolution_multiply_fusion.2
  71.0 1.0 convolution_multiply_fusion.1
  72.1 1.0 convolution_multiply_fusion
  73.1 79.0 %all-gather.6.cloned.1.call-done = f32[8192,128]{1,0:T(8,128)} async-done(((f32[128,128]{1,0:T(8,128)}), f32[8192,128]{1,0:T(8,128)}) %all-gather.6.cloned.1.call-update) | async-done | bytes 4194320 | tf_op jit(solution)/shard_map/all_gather | solution.py:48
  152.1 2.5 reduce_sum.9
  154.7 11.9 %cholesky.20 = f32[128,128]{1,0:T(8,128)S(1)} custom-call(f32[128,128]{1,0:T(8,128)S(1)} %fusion.3), custom_call_target="Cholesky" | custom-call | tf_op jit(solution)/shard_map/jit(cholesky)/cholesky | solution.py:49
  168.0 9.8 %custom-call.7 = f32[1,128,128]{1,2,0:T(8,128)S(1)} custom-call(f32[1,128,128]{2,1,0:T(8,128)S(1)} %get-tuple-element.105), custom_call_target="InvertDiagBlocksLowerTriangular" | custom-call | tf_op jit(solution)/shard_map/jit(_solve_triangular)/triangular_solve | solution.py:50
  178.1 1.0 fusion.37
  179.1 1.0 copy-done.1
  180.1 1.8 fusion.38
  182.6 181.0 %all-reduce.2.cloned.1.call-done = f32[128,256]{1,0:T(8,128)} async-done(((f32[128,256]{1,0:T(8,128)}), f32[128,256]{1,0:T(8,128)}) %all-reduce.2.cloned.1.call-update) | async-done | bytes 131088 | tf_op jit(solution)/shard_map/psum | solution.py:55
  363.6 4.4 %fusion = f32[2048,256]{1,0:T(8,128)} fusion(f32[2048,256]{1,0:T(8,128)S(1)} %convolution_multiply_fusion, f32[128,2048]{1,0:T(8,128)} %copy-done.1, f32[128,256]{1,0:T(8,128)} %all-reduce.2.cloned.1.call-done), kind=kOutput, calls=%fused_computation.11 | convolution fusion | flops 806354944 | bytes 5373952 | tf_op jit(solution)/shard_map/dot_general | solution.py:37
  (59 shorter events, 8.6 us)
Async XLA Ops:
  7.2 51.8 %all-gather.4.cloned.1.call-start = ((), (), s32[]{:S(2)}) async-start(), calls=%async_computation | async-start | bytes 1179648 | tf_op jit(solution)/shard_map/all_gather | solution.py:44
  15.1 47.4 %copy-start.3 = (s32[10,256]{1,0:T(8,128)S(1)}, s32[10,256]{1,0:T(8,128)}, u32[]{:S(2)}) copy-start(s32[10,256]{1,0:T(8,128)} %param.7) | copy-start | bytes 30724
  17.2 134.9 %all-gather.6.cloned.1.call-start = ((), (), s32[]{:S(2)}) async-start(), calls=%async_computation.2 | async-start | bytes 4259840 | tf_op jit(solution)/shard_map/all_gather | solution.py:48
  62.2 301.5 %all-reduce.2.cloned.1.call-start = ((), (), s32[]{:S(2)}) async-start(), calls=%async_computation.1 | async-start | bytes 262144 | tf_op jit(solution)/shard_map/psum | solution.py:55
  152.1 25.9 %copy-start = (f32[2048,128]{0,1:T(8,128)S(1)}, f32[2048,128]{0,1:T(8,128)}, u32[]{:S(2)}) copy-start(f32[2048,128]{0,1:T(8,128)} %all-gather.4.cloned.1.call-done) | copy-start | bytes 3145732
  179.1 1.0 copy-start.1
  363.6 4.4 %copy-start.2 = (f32[128,256]{1,0:T(8,128)S(1)}, f32[128,256]{1,0:T(8,128)}, u32[]{:S(2)}) copy-start(f32[128,256]{1,0:T(8,128)} %all-reduce.2.cloned.1.call-done) | copy-start | bytes 393220
Sparse Core Ops, SparseCore 0:
  17.3 41.6 all-gather.3
  62.9 89.1 all-gather.5
  182.0 181.5 all-reduce.1
